TPU v7x, 32 devices: a whole 2x2x4 slice. The times are simulated.
32 devices in a mesh: groups: 2 (over x), expert: 8 (over z, y), hidden: 2 (over core).
Axes of the slice: x: 2, y: 2, z: 4, core: 2. Of those that a mesh axis runs over, the one named last changes fastest.
Arguments:
- tokens: bfloat16 [4096, 768], P(('groups', 'expert', 'hidden')), parts along dimension 0, may hold values from -6 to 6
- grad_out: bfloat16 [4096, 768], P(('groups', 'expert', 'hidden')), parts along dimension 0, may hold values from -24 to 24
- probs: float32 [4096, 8], P(('groups', 'expert', 'hidden')), parts along dimension 0, may hold values from 0 to 1, as said below
- choices: int32 [16, 256], P('groups'), parts along dimension 0, may hold values from 0 to 2047, as said below
- w_in: bfloat16 [8, 768, 3072], P('expert', None, 'hidden'), may hold values from -0.21875 to 0.21875
- w_out: bfloat16 [8, 3072, 768], P('expert', 'hidden'), may hold values from -0.109375 to 0.109375
- router: float32 [768, 8], replicated, may hold values from -0.0546875 to 0.0546875
Outputs:
- grad_tokens: bfloat16 [4096, 768], P(('groups', 'expert', 'hidden')), parts along dimension 0
- grad_w_in: bfloat16 [16, 768, 3072], P(('groups', 'expert'), None, 'hidden'), parts along dimension 0
- grad_w_out: bfloat16 [16, 3072, 768], P(('groups', 'expert'), 'hidden'), parts along dimension 0
- grad_logits: float32 [4096, 8], P(('groups', 'expert', 'hidden')), parts along dimension 0
There are 2 independent parts, one for each index of `groups`. A program takes and returns all parts, laid end to end along the dimension named above; an argument that names none is the same for every part. Nothing has to cross between parts.
Inputs may be any that keep to these rules, and one draw needn't show every extreme that they name: `choices`: every row holds 256 distinct token indices in ascending order. At most 32 entries of one row lie among the tokens of one device (indices k * 128 to (k + 1) * 128 - 1), and every row has exactly 32 on some device. `probs`: each row is positive and sums to one.
All inputs are finite; a program needn't handle non-finite values.
Results may differ from a plain program's by a relative error of at most 0.0065.
Values may be sent and summed in bfloat16 or wider, within the bound.
A program may use at most 64 MiB of HBM per device.

v0:
```python
import math

import jax
import jax.numpy as jnp
from jax import lax
from jax.sharding import PartitionSpec as P

gelu_scale = math.sqrt(2.0 / math.pi)
cubic_coef = 0.044715


def gelu_parts(inputs):
    tanh_value = jnp.tanh(gelu_scale * (inputs + cubic_coef * inputs * inputs * inputs))
    gelu_value = 0.5 * inputs * (1.0 + tanh_value)
    gelu_slope = 0.5 * (1.0 + tanh_value) + 0.5 * inputs * (
        1.0 - tanh_value * tanh_value
    ) * gelu_scale * (1.0 + 3.0 * cubic_coef * inputs * inputs)
    return (gelu_value, gelu_slope)


def expert_pass(token_rows, grad_rows, gate_rows, w_first, w_second):
    leading = token_rows.shape[:-1]
    width = token_rows.shape[-1]
    flat_tokens = token_rows.reshape(-1, width)
    flat_grads = grad_rows.reshape(-1, width)
    flat_gates = gate_rows.reshape(-1)
    pre_act = jnp.dot(flat_tokens, w_first, preferred_element_type=jnp.float32)
    gelu_value, gelu_slope = gelu_parts(pre_act)
    activation = gelu_value.astype(jnp.bfloat16)
    branch_out = jnp.dot(activation, w_second, preferred_element_type=jnp.float32)
    gate_grad = jnp.sum(flat_grads.astype(jnp.float32) * branch_out, axis=-1)
    scaled_grad = (flat_gates.astype(jnp.float32)[:, None] * flat_grads.astype(jnp.float32)).astype(
        jnp.bfloat16
    )
    act_grad = lax.dot_general(
        scaled_grad, w_second, (((1,), (1,)), ((), ())), preferred_element_type=jnp.float32
    )
    pre_grad = (act_grad * gelu_slope).astype(jnp.bfloat16)
    input_part = lax.dot_general(
        pre_grad, w_first, (((1,), (1,)), ((), ())), preferred_element_type=jnp.float32
    )
    hidden_width = w_first.shape[1]
    return (
        input_part.reshape(leading + (width,)),
        gate_grad.reshape(leading),
        token_rows,
        activation.reshape(leading + (hidden_width,)),
        scaled_grad.reshape(leading + (width,)),
        pre_grad.reshape(leading + (hidden_width,)),
    )


def body(tokens, grad_out, probs, choices, w_in, w_out, router):
    tok_dev, width = tokens.shape
    experts, capacity = choices.shape
    expert_count = lax.axis_size("expert")
    hidden_count = lax.axis_size("hidden")
    owner_count = expert_count * hidden_count
    slot_count = 2 * capacity // owner_count
    slot_total = experts * slot_count
    my_owner = lax.axis_index("expert") * hidden_count + lax.axis_index("hidden")
    w_first = w_in[0]
    w_second = w_out[0]
    owners_of = choices // tok_dev
    before = jnp.sum((owners_of < my_owner).astype(jnp.int32), axis=1)
    mine_count = jnp.sum((owners_of == my_owner).astype(jnp.int32), axis=1)
    slot_rank = lax.broadcasted_iota(jnp.int32, (experts, slot_count), 1)
    position = before[:, None] + slot_rank
    pick_mask = (
        lax.broadcasted_iota(jnp.int32, (experts, slot_count, capacity), 2) == position[:, :, None]
    )
    picked = jnp.sum(jnp.where(pick_mask, choices[:, None, :], 0), axis=2)
    slot_token = jnp.where(
        slot_rank < mine_count[:, None], picked - my_owner * tok_dev, tok_dev
    ).reshape(-1)
    slot_expert = lax.broadcasted_iota(jnp.int32, (experts, slot_count), 0).reshape(-1)
    selector = slot_token[:, None] == lax.broadcasted_iota(jnp.int32, (slot_total, tok_dev), 1)
    select_half = selector.astype(jnp.bfloat16)
    select_full = selector.astype(jnp.float32)
    expert_mask = slot_expert[:, None] == lax.broadcasted_iota(jnp.int32, (slot_total, experts), 1)
    stacked = jnp.concatenate([tokens, grad_out], axis=1)
    picked_rows = jnp.dot(select_half, stacked, preferred_element_type=jnp.float32).astype(
        jnp.bfloat16
    )
    send_tokens = picked_rows[:, :width].reshape(experts, slot_count, width)
    send_grads = picked_rows[:, width:].reshape(experts, slot_count, width)
    prob_rows = jnp.dot(
        select_full, probs, precision=lax.Precision.HIGHEST, preferred_element_type=jnp.float32
    )
    send_gates = (
        jnp.sum(jnp.where(expert_mask, prob_rows, 0.0), axis=1)
        .astype(jnp.bfloat16)
        .reshape(experts, slot_count)
    )

    def doubled(array):
        spread = jnp.broadcast_to(array[:, None], (experts, hidden_count) + array.shape[1:])
        return spread.reshape((experts * hidden_count,) + array.shape[1:])

    results = expert_pass(
        lax.all_to_all(
            doubled(send_tokens), ("expert", "hidden"), split_axis=0, concat_axis=0, tiled=True
        ),
        lax.all_to_all(
            doubled(send_grads), ("expert", "hidden"), split_axis=0, concat_axis=0, tiled=True
        ),
        lax.all_to_all(
            doubled(send_gates), ("expert", "hidden"), split_axis=0, concat_axis=0, tiled=True
        ),
        w_first,
        w_second,
    )
    input_part, gate_part, token_rows, activation, scaled_grad, pre_grad = results
    hidden_width = w_first.shape[1]
    grad_first = lax.dot_general(
        token_rows.reshape(-1, width),
        pre_grad.reshape(-1, hidden_width),
        (((0,), (0,)), ((), ())),
        preferred_element_type=jnp.float32,
    )
    grad_second = lax.dot_general(
        activation.reshape(-1, hidden_width),
        scaled_grad.reshape(-1, width),
        (((0,), (0,)), ((), ())),
        preferred_element_type=jnp.float32,
    )
    grad_w_in = grad_first.astype(jnp.bfloat16)[None]
    grad_w_out = grad_second.astype(jnp.bfloat16)[None]
    back_rows, back_gates = (
        lax.all_to_all(input_part, ("expert", "hidden"), split_axis=0, concat_axis=0, tiled=True),
        lax.all_to_all(gate_part, ("expert", "hidden"), split_axis=0, concat_axis=0, tiled=True),
    )
    rows_back = jnp.sum(back_rows.reshape(experts, hidden_count, slot_count, width), axis=1)
    gates_back = jnp.sum(back_gates.reshape(experts, hidden_count, slot_count), axis=1)
    moe_grad = lax.dot_general(
        select_full,
        rows_back.reshape(slot_total, width),
        (((0,), (0,)), ((), ())),
        precision=lax.Precision.HIGHEST,
        preferred_element_type=jnp.float32,
    )
    gate_table = jnp.where(expert_mask, gates_back.reshape(-1)[:, None], 0.0)
    score_grad = lax.dot_general(
        select_full,
        gate_table,
        (((0,), (0,)), ((), ())),
        precision=lax.Precision.HIGHEST,
        preferred_element_type=jnp.float32,
    )
    grad_logits = probs * (score_grad - jnp.sum(probs * score_grad, axis=-1, keepdims=True))
    router_part = lax.dot_general(
        grad_logits,
        router,
        (((1,), (1,)), ((), ())),
        precision=lax.Precision.HIGHEST,
        preferred_element_type=jnp.float32,
    )
    grad_tokens = (moe_grad + router_part).astype(jnp.bfloat16)
    return (grad_tokens, grad_w_in, grad_w_out, grad_logits)


def solution(mesh):
    in_specs = (
        P(("groups", "expert", "hidden"), None),
        P(("groups", "expert", "hidden"), None),
        P(("groups", "expert", "hidden"), None),
        P("groups", None),
        P("expert", None, "hidden"),
        P("expert", "hidden", None),
        P(),
    )
    out_specs = (
        P(("groups", "expert", "hidden"), None),
        P(("groups", "expert"), None, "hidden"),
        P(("groups", "expert"), "hidden", None),
        P(("groups", "expert", "hidden"), None),
    )
    return jax.shard_map(body, mesh=mesh, in_specs=in_specs, out_specs=out_specs, check_vma=False)
```

profile of v0, /device:TPU:19, one launch (start us, length us, event | category | flops | bytes accessed | tf_op | source)
XLA Modules:
  0.0 129.6 jit_solution(8614208847361260247)
XLA Ops:
  0.6 0.0 copy-start
  0.7 1.0 convert_reduce_fusion.1
  1.6 0.1 iota_add_fusion
  1.7 1.0 select_reduce_fusion
  2.7 0.1 subtract_select_fusion
  2.8 0.1 select_n.31
  2.9 0.1 eq.44
  3.0 1.0 fusion.21
  3.9 0.1 convert_element_type.73
  4.0 0.6 copy.15
  4.6 6.5 %all-to-all-start = ((bf16[16,1,32]{2,1,0:T(2,128)(2,1)}), bf16[16,1,32]{2,1,0:T(2,128)(2,1)S(1)}, u32[]{:S(2)}, u32[]{:S(2)}) async-start(bf16[16,1,32]{2,1,0:T(2,128)(2,1)} %copy.15), calls=%async_computation | async-start | bytes 16384 | tf_op jit(solution)/shard_map/all_to_all | solution.py:107
  11.1 1.4 %convolution_convert_fusion.2 = bf16[256,1536]{1,0:T(8,128)(2,1)S(1)} fusion(bf16[128,768]{1,0:T(8,128)(2,1)} %param.8, bf16[128,768]{1,0:T(8,128)(2,1)} %param.7, s32[256]{0:T(256)S(1)} %select_n.31), kind=kOutput, calls=%fused_computation.14 | convolution fusion | flops 101875712 | bytes 1180672 | tf_op jit(solution)/shard_map/dot_general | solution.py:82
  12.6 0.1 fusion.39
  12.6 2.2 %all-to-all-done = bf16[16,1,32]{2,1,0:T(2,128)(2,1)S(1)} async-done(((bf16[16,1,32]{2,1,0:T(2,128)(2,1)}), bf16[16,1,32]{2,1,0:T(2,128)(2,1)S(1)}, u32[]{:S(2)}, u32[]{:S(2)}) %all-to-all-start) | async-done | bytes 1056 | tf_op jit(solution)/shard_map/all_to_all | solution.py:107
  14.9 0.1 broadcast_in_dim.71
  14.9 24.7 %all_to_all.33 = bf16[16,32,768]{2,1,0:T(8,128)(2,1)} all-to-all(bf16[16,32,768]{2,1,0:T(8,128)(2,1)S(1)} %bitcast.48), channel_id=1, replica_groups=mesh['groups'=2,'expert'=8,'hidden'=2] {'expert','hidden'}, dimensions={0} | all-to-all | bytes 1572864 | tf_op jit(solution)/shard_map/all_to_all | solution.py:101
  39.6 1.0 broadcast_in_dim.69
  40.6 5.3 %all-to-all-start.1 = ((bf16[16,32,768]{2,1,0:T(8,128)(2,1)}), bf16[16,32,768]{2,1,0:T(8,128)(2,1)S(1)}, u32[]{:S(2)}, u32[]{:S(2)}) async-start(bf16[16,32,768]{2,1,0:T(8,128)(2,1)} %bitcast.47), calls=%async_computation.1 | async-start | bytes 1572864 | tf_op jit(solution)/shard_map/all_to_all | solution.py:104
  45.9 0.0 copy-done
  45.9 4.2 %fusion.10 = f32[512,1536]{1,0:T(8,128)} fusion(bf16[512,768]{1,0:T(8,128)(2,1)} %bitcast.52, bf16[1,768,1536]{2,1,0:T(8,128)(2,1)S(1)} %copy-done), kind=kOutput, calls=%fused_computation.17 | convolution fusion | flops 1207959552 | bytes 6291456 | tf_op jit(solution)/shard_map/dot_general | solution.py:27
  50.1 14.8 %all-to-all-done.1 = bf16[16,32,768]{2,1,0:T(8,128)(2,1)S(1)} async-done(((bf16[16,32,768]{2,1,0:T(8,128)(2,1)}), bf16[16,32,768]{2,1,0:T(8,128)(2,1)S(1)}, u32[]{:S(2)}, u32[]{:S(2)}) %all-to-all-start.1) | async-done | bytes 786464 | tf_op jit(solution)/shard_map/all_to_all | solution.py:104
  65.0 4.7 %fusion.16 = f32[512]{0:T(512)S(1)} fusion(bf16[16,32,768]{2,1,0:T(8,128)(2,1)S(1)} %all-to-all-done.1, bf16[1,1536,768]{2,1,0:T(8,128)(2,1)} %param.12, f32[512,1536]{1,0:T(8,128)} %fusion.10), kind=kOutput, calls=%fused_computation.26 | convolution fusion | flops 1216216576 | bytes 6293504 | tf_op jit(solution)/shard_map/dot_general | solution.py:30
  69.6 0.7 all_to_all.26
  70.3 5.1 %all-to-all-start.4 = ((f32[16,1,32]{2,1,0:T(1,128)}), f32[16,1,32]{2,1,0:T(1,128)S(1)}, u32[]{:S(2)}, u32[]{:S(2)}) async-start(f32[16,1,32]{2,1,0:T(1,128)} %all_to_all.26), calls=%async_computation.4 | async-start | bytes 16384 | tf_op jit(solution)/shard_map/all_to_all | solution.py:131
  75.4 0.2 fusion.15
  75.6 4.8 %fusion.7 = bf16[512,1536]{1,0:T(8,128)(2,1)S(1)} fusion(f32[512,1536]{1,0:T(8,128)} %fusion.10, bf16[512,768]{1,0:T(8,128)(2,1)S(1)} %bitcast.54, bf16[1,1536,768]{2,1,0:T(8,128)(2,1)} %param.12), kind=kOutput, calls=%fused_computation.13 | convolution fusion | flops 1222901760 | bytes 7864320 | tf_op jit(solution)/shard_map/dot_general | solution.py:35
  80.5 0.0 copy-start.4
  80.5 1.1 copy-done.4
  81.6 2.6 %fusion.8 = f32[16,32,768]{2,1,0:T(8,128)} fusion(bf16[16,32,1536]{2,1,0:T(8,128)(2,1)S(1)} %bitcast.58, bf16[1,768,1536]{2,1,0:T(8,128)(2,1)S(1)} %copy-done), kind=kOutput, calls=%fused_computation.15 | convolution fusion | flops 1207959552 | bytes 5505024 | tf_op jit(solution)/shard_map/dot_general | solution.py:39
  84.2 0.0 all-to-all-done.4
  84.2 6.0 %all-to-all-start.3 = ((f32[16,32,768]{2,1,0:T(8,128)}), f32[16,32,768]{2,1,0:T(8,128)}, u32[]{:S(2)}, u32[]{:S(2)}) async-start(f32[16,32,768]{2,1,0:T(8,128)} %fusion.8), calls=%async_computation.3 | async-start | bytes 3145728 | tf_op jit(solution)/shard_map/all_to_all | solution.py:130
  90.3 0.1 reshape.123
  90.4 0.2 fusion.17
  90.6 0.0 copy-start.5
  90.6 4.6 %fusion.5 = bf16[1,768,1536]{2,1,0:T(8,128)(2,1)} fusion(bf16[512,768]{1,0:T(8,128)(2,1)} %bitcast.53, bf16[512,1536]{1,0:T(8,128)(2,1)} %copy-done.4), kind=kOutput, calls=%fused_computation.11 | convolution fusion | flops 1209139200 | bytes 4718592 | tf_op jit(solution)/shard_map/dot_general | solution.py:115
  95.2 0.0 copy-done.5
  95.2 0.0 copy-start.3
  95.2 3.2 %fusion.6 = bf16[1,1536,768]{2,1,0:T(8,128)(2,1)} fusion(bf16[512,768]{1,0:T(8,128)(2,1)S(1)} %fusion.17, f32[512,1536]{1,0:T(8,128)S(1)} %copy-done.5), kind=kOutput, calls=%fused_computation.12 | convolution fusion | flops 1216217088 | bytes 6291456 | tf_op jit(solution)/shard_map/dot_general | solution.py:121
  98.4 0.1 broadcast_in_dim.72
  98.5 0.0 copy-done.3
  98.5 0.2 multiply_reduce_fusion
  98.7 0.0 copy-start.2
  98.7 27.5 %all-to-all-done.3 = f32[16,32,768]{2,1,0:T(8,128)} async-done(((f32[16,32,768]{2,1,0:T(8,128)}), f32[16,32,768]{2,1,0:T(8,128)}, u32[]{:S(2)}, u32[]{:S(2)}) %all-to-all-start.3) | async-done | bytes 1572896 | tf_op jit(solution)/shard_map/all_to_all | solution.py:130
  126.3 1.6 %bitcast_reduce_fusion = f32[8,32,768]{2,1,0:T(8,128)S(1)} fusion(f32[16,32,768]{2,1,0:T(8,128)} %all-to-all-done.3), kind=kLoop, calls=%fused_computation.28 | loop fusion | flops 196608 | bytes 2359296 | tf_op jit(solution)/shard_map/reduce_sum | solution.py:133
  127.9 0.5 fusion.26
  128.4 0.0 copy-done.1
  128.4 1.2 fusion.20
  129.6 0.0 copy-done.2
  (7 shorter events, 0.1 us)
Async XLA Ops:
  0.6 45.3 %copy-start = (bf16[1,768,1536]{2,1,0:T(8,128)(2,1)S(1)}, bf16[1,768,1536]{2,1,0:T(8,128)(2,1)}, u32[]{:S(2)}) copy-start(bf16[1,768,1536]{2,1,0:T(8,128)(2,1)} %param.11) | copy-start | bytes 7077892
  4.6 10.2 %all-to-all-start = ((bf16[16,1,32]{2,1,0:T(2,128)(2,1)}), bf16[16,1,32]{2,1,0:T(2,128)(2,1)S(1)}, u32[]{:S(2)}, u32[]{:S(2)}) async-start(bf16[16,1,32]{2,1,0:T(2,128)(2,1)} %copy.15), calls=%async_computation | async-start | bytes 16384 | tf_op jit(solution)/shard_map/all_to_all | solution.py:107
  40.6 24.4 %all-to-all-start.1 = ((bf16[16,32,768]{2,1,0:T(8,128)(2,1)}), bf16[16,32,768]{2,1,0:T(8,128)(2,1)S(1)}, u32[]{:S(2)}, u32[]{:S(2)}) async-start(bf16[16,32,768]{2,1,0:T(8,128)(2,1)} %bitcast.47), calls=%async_computation.1 | async-start | bytes 1572864 | tf_op jit(solution)/shard_map/all_to_all | solution.py:104
  70.3 13.9 %all-to-all-start.4 = ((f32[16,1,32]{2,1,0:T(1,128)}), f32[16,1,32]{2,1,0:T(1,128)S(1)}, u32[]{:S(2)}, u32[]{:S(2)}) async-start(f32[16,1,32]{2,1,0:T(1,128)} %all_to_all.26), calls=%async_computation.4 | async-start | bytes 16384 | tf_op jit(solution)/shard_map/all_to_all | solution.py:131
  80.5 1.1 copy-start.4
  84.2 42.0 %all-to-all-start.3 = ((f32[16,32,768]{2,1,0:T(8,128)}), f32[16,32,768]{2,1,0:T(8,128)}, u32[]{:S(2)}, u32[]{:S(2)}) async-start(f32[16,32,768]{2,1,0:T(8,128)} %fusion.8), calls=%async_computation.3 | async-start | bytes 3145728 | tf_op jit(solution)/shard_map/all_to_all | solution.py:130
  90.6 4.6 %copy-start.5 = (f32[512,1536]{1,0:T(8,128)S(1)}, f32[512,1536]{1,0:T(8,128)}, u32[]{:S(2)}) copy-start(f32[512,1536]{1,0:T(8,128)} %fusion.10) | copy-start | bytes 9437188
  95.2 3.3 %copy-start.3 = (f32[128,8]{0,1:T(8,128)S(1)}, f32[128,8]{0,1:T(8,128)}, u32[]{:S(2)}) copy-start(f32[128,8]{0,1:T(8,128)} %param.9) | copy-start | bytes 12292
  98.4 30.0 %copy-start.1 = (f32[768,8]{0,1:T(8,128)S(1)}, f32[768,8]{0,1:T(8,128)}, u32[]{:S(2)}) copy-start(f32[768,8]{0,1:T(8,128)} %param.13) | copy-start | bytes 73732
  98.7 30.9 %copy-start.2 = (f32[128,8]{0,1:T(8,128)}, f32[128,8]{0,1:T(8,128)S(1)}, u32[]{:S(2)}) copy-start(f32[128,8]{0,1:T(8,128)S(1)} %subtract_multiply_fusion) | copy-start | bytes 12292
where the time goes:
time: 130 us
  waiting for transfers between devices  44.6 us (34%)
  matrix products  28.4 us (22%)
  blocking collectives  24.7 us (19%)
  starting transfers between devices  23 us (18%)
  other arithmetic  4.23 us (3%)
  local copies, waits for them, and re-layouts  3.97 us (3%)
    all_to_all x1, waiting for transfers between devices, body(): lax.all_to_all(input_part, ('expert', 'hidden'), split_axis=0, concat_axi...  27.5 us
    all_to_all x1, blocking collectives, body(): lax.all_to_all(doubled(send_tokens), ('expert', 'hidden'), split_axis=0,...  24.7 us
    all_to_all x1, waiting for transfers between devices, body(): lax.all_to_all(doubled(send_grads), ('expert', 'hidden'), split_axis=0, c...  14.8 us
    all_to_all x1, starting transfers between devices, body(): lax.all_to_all(doubled(send_gates), ('expert', 'hidden'), split_axis=0, c...  6.5 us
    all_to_all x1, starting transfers between devices, body(): lax.all_to_all(input_part, ('expert', 'hidden'), split_axis=0, concat_axi...  6.02 us
    all_to_all x1, starting transfers between devices, body(): lax.all_to_all(doubled(send_grads), ('expert', 'hidden'), split_axis=0, c...  5.33 us
    all_to_all x1, starting transfers between devices, body(): lax.all_to_all(gate_part, ('expert', 'hidden'), split_axis=0, concat_axis...  5.13 us
    dot_general x1, matrix products, expert_pass(): lax.dot_general(scaled_grad, w_second, (((1,), (1,)), ((), ())), preferre...  4.84 us
  transfers between devices with their start and end apart: 4, of which 3 were waited for; matrix products, arithmetic and copies ran while one was open for 17% of the time, Pallas kernels for 0%

commit v1 on v0

--- a/solution.py
+++ b/solution.py
@@ -1,8 +1,11 @@
+import functools
 import math
 
 import jax
 import jax.numpy as jnp
 from jax import lax
+from jax.experimental import pallas as pl
+from jax.experimental.pallas import tpu as pltpu
 from jax.sharding import PartitionSpec as P
 
 gelu_scale = math.sqrt(2.0 / math.pi)
@@ -50,7 +53,7 @@
     )
 
 
-def body(tokens, grad_out, probs, choices, w_in, w_out, router):
+def general_body(tokens, grad_out, probs, choices, w_in, w_out, router):
     tok_dev, width = tokens.shape
     experts, capacity = choices.shape
     expert_count = lax.axis_size("expert")
@@ -159,6 +162,381 @@
     return (grad_tokens, grad_w_in, grad_w_out, grad_logits)
 
 
+MESH = pl.DeviceIdType.MESH
+
+
+def matmul(a, b, contract):
+    return lax.dot_general(a, b, (contract, ((), ())), preferred_element_type=jnp.float32)
+
+
+NN = ((1,), (0,))
+NT = ((1,), (1,))
+TN = ((0,), (0,))
+
+
+def fused_kernel(
+    experts,
+    slots,
+    tile,
+    tokens_ref,
+    grads_ref,
+    probs_ref,
+    choices_ref,
+    router_ref,
+    w_in_hbm,
+    w_out_hbm,
+    grad_tokens_ref,
+    grad_logits_ref,
+    grad_w_in_hbm,
+    grad_w_out_hbm,
+    w_in_ref,
+    w_out_ref,
+    select_ref,
+    send_ref,
+    rows_ref,
+    scaled_ref,
+    act_ref,
+    pre_grad_ref,
+    part_ref,
+    pair_ref,
+    ret_ref,
+    back_ref,
+    first_ref,
+    second_ref,
+    weight_sem,
+    go_send,
+    go_recv,
+    fwd_send,
+    fwd_recv,
+    pair_send,
+    pair_recv,
+    ret_send,
+    ret_recv,
+    first_sem,
+    second_sem,
+):
+    tok_dev, width = tokens_ref.shape
+    hidden = w_in_ref.shape[1]
+    half = experts // 2
+    chunk = half * slots
+    me = lax.axis_index("expert")
+    core = lax.axis_index("hidden")
+    base = (me * 2 + core) * tok_dev
+    side = me // half
+    place = me % half
+
+    def target(step):
+        where = side if step < half else 1 - side
+        return where * half + (place + step) % half
+
+    def source(step):
+        where = side if step < half else 1 - side
+        return where * half + (place + 2 * half - step) % half
+
+    def direct_row(step):
+        return (step // half) * 2 * chunk + (step % half) * slots
+
+    sibling = {"hidden": 1 - core}
+    barrier = pltpu.get_barrier_semaphore()
+    for step in range(1, experts):
+        pl.semaphore_signal(
+            barrier, inc=1, device_id={"expert": target(step)}, device_id_type=MESH
+        )
+    pl.semaphore_signal(barrier, inc=1, device_id=sibling, device_id_type=MESH)
+    load_in = pltpu.make_async_copy(w_in_hbm.at[0], w_in_ref, weight_sem.at[0])
+    load_out = pltpu.make_async_copy(w_out_hbm.at[0], w_out_ref, weight_sem.at[1])
+    load_in.start()
+    load_out.start()
+
+    def go_copy(step):
+        return pltpu.make_async_remote_copy(
+            src_ref=send_ref.at[pl.ds(step * slots, slots)],
+            dst_ref=rows_ref.at[pl.ds(direct_row(step), slots)],
+            send_sem=go_send.at[step],
+            recv_sem=go_recv.at[step],
+            device_id={"expert": target(step)},
+            device_id_type=MESH,
+        )
+
+    def fwd_copy(step):
+        return pltpu.make_async_remote_copy(
+            src_ref=rows_ref.at[pl.ds(direct_row(step), slots)],
+            dst_ref=rows_ref.at[pl.ds(direct_row(step) + chunk, slots)],
+            send_sem=fwd_send.at[step],
+            recv_sem=fwd_recv.at[step],
+            device_id=sibling,
+            device_id_type=MESH,
+        )
+
+    def pair_copy(part):
+        return pltpu.make_async_remote_copy(
+            src_ref=part_ref.at[part, pl.ds(chunk, chunk)],
+            dst_ref=pair_ref.at[part],
+            send_sem=pair_send.at[part],
+            recv_sem=pair_recv.at[part],
+            device_id=sibling,
+            device_id_type=MESH,
+        )
+
+    def ret_copy(step):
+        return pltpu.make_async_remote_copy(
+            src_ref=ret_ref.at[pl.ds(step * slots, slots)],
+            dst_ref=back_ref.at[pl.ds(step * slots, slots)],
+            send_sem=ret_send.at[step],
+            recv_sem=ret_recv.at[step],
+            device_id={"expert": source(step)},
+            device_id_type=MESH,
+        )
+
+    probs = probs_ref[...]
+    probs_half = probs.astype(jnp.bfloat16)
+    capacity = choices_ref.shape[1]
+    rank_gap = lax.broadcasted_iota(jnp.int32, (slots, capacity), 1) - lax.broadcasted_iota(
+        jnp.int32, (slots, capacity), 0
+    )
+    rank_gap = rank_gap.astype(jnp.float32)
+    token_id = lax.broadcasted_iota(jnp.int32, (tok_dev, capacity), 0) + base
+    column = lax.broadcasted_iota(jnp.int32, (slots, experts), 1)
+
+    def select(part):
+        for step in range(part * half, (part + 1) * half):
+            row = choices_ref[pl.ds(target(step), 1), :]
+            before = jnp.sum(jnp.where(row < base, 1.0, 0.0), axis=1, keepdims=True)
+            pick = jnp.where(rank_gap == before, 1.0, 0.0).astype(jnp.bfloat16)
+            equal = jnp.where(token_id == row, 1.0, 0.0).astype(jnp.bfloat16)
+            select_ref[pl.ds(step * slots, slots), :] = matmul(pick, equal, NT).astype(jnp.bfloat16)
+        chosen = select_ref[pl.ds(part * chunk, chunk), :]
+        token_rows = matmul(chosen, tokens_ref[...], NN).astype(jnp.bfloat16)
+        grad_rows = matmul(chosen, grads_ref[...], NN).astype(jnp.bfloat16)
+        gates = matmul(chosen, probs_half, NN)
+        for index in range(half):
+            step = part * half + index
+            mine = slice(index * slots, (index + 1) * slots)
+            gate = jnp.sum(
+                jnp.where(column == target(step), gates[mine], 0.0), axis=1, keepdims=True
+            )
+            gate = jnp.broadcast_to(gate, (slots, 128)).astype(jnp.bfloat16)
+            ref = rows_ref if step == 0 else send_ref
+            at = pl.ds(step * slots, slots)
+            ref[at, :width] = token_rows[mine]
+            ref[at, width : 2 * width] = grad_rows[mine]
+            ref[at, 2 * width :] = gate
+
+    select(1)
+    pl.semaphore_wait(barrier, experts)
+    for step in range(half, experts):
+        go_copy(step).start()
+    select(0)
+    for step in range(1, half):
+        go_copy(step).start()
+
+    def forward(part):
+        for step in range(part * half, (part + 1) * half):
+            if step:
+                go_copy(step).wait_recv()
+            fwd_copy(step).start()
+
+    def compute(part):
+        for step in range(part * half, (part + 1) * half):
+            fwd_copy(step).wait_recv()
+        rows = pl.ds(part * 2 * chunk, 2 * chunk)
+        gate = rows_ref[rows, 2 * width :].astype(jnp.float32)
+        wide_gate = jnp.concatenate([gate] * (width // 128), axis=1)
+        scaled_ref[rows, :] = (
+            wide_gate * rows_ref[rows, width : 2 * width].astype(jnp.float32)
+        ).astype(jnp.bfloat16)
+        part_ref[part] = jnp.zeros(part_ref.shape[1:], jnp.float32)
+
+        def step_tile(index, carry):
+            at = pl.ds(pl.multiple_of(index * tile, tile), tile)
+            w_first = w_in_ref[:, at]
+            w_second = w_out_ref[at, :]
+            pre_act = matmul(rows_ref[rows, :width], w_first, NN)
+            raw_grad = matmul(rows_ref[rows, width : 2 * width], w_second, NT)
+            gelu_value, gelu_slope = gelu_parts(pre_act)
+            act = gelu_value.astype(jnp.bfloat16)
+            act_ref[rows, at] = act
+            product = act.astype(jnp.float32) * raw_grad
+            gate_tile = jnp.concatenate([gate] * (tile // 128), axis=1)
+            pre_grad = (gate_tile * raw_grad * gelu_slope).astype(jnp.bfloat16)
+            pre_grad_ref[rows, at] = pre_grad
+            part_ref[part, :, :width] += matmul(pre_grad, w_first, NT)
+            total = product[:, :128]
+            for lane in range(128, tile, 128):
+                total = total + product[:, lane : lane + 128]
+            part_ref[part, :, width:] += total
+            return carry
+
+        lax.fori_loop(0, hidden // tile, step_tile, 0)
+        pair_copy(part).start()
+
+    lane = lax.broadcasted_iota(jnp.int32, (chunk, 128), 1)
+
+    def give_back(part):
+        pair_copy(part).wait_recv()
+        total = part_ref[part, :chunk, :] + pair_ref[part]
+        gate_grad = jnp.sum(total[:, width:], axis=1, keepdims=True)
+        high = gate_grad.astype(jnp.bfloat16).astype(jnp.float32)
+        low = gate_grad - high
+        coded = jnp.where(lane == me, high, jnp.where(lane == me + experts, low, 0.0))
+        values = total[:, :width].astype(jnp.bfloat16)
+        coded = coded.astype(jnp.bfloat16)
+        for index in range(half):
+            step = part * half + index
+            mine = slice(index * slots, (index + 1) * slots)
+            ref = ret_ref if step else back_ref
+            ref[pl.ds(step * slots, slots), :width] = values[mine]
+            ref[pl.ds(step * slots, slots), width:] = coded[mine]
+            if step:
+                ret_copy(step).start()
+
+    first_rows = 256
+    second_rows = 256
+
+    def first_out(index):
+        at = pl.ds(pl.multiple_of(index * first_rows, first_rows), first_rows)
+        return pltpu.make_async_copy(
+            first_ref.at[at], grad_w_in_hbm.at[0, at], first_sem.at[index]
+        )
+
+    def second_out(index):
+        at = pl.ds(pl.multiple_of(index * second_rows, second_rows), second_rows)
+        return pltpu.make_async_copy(
+            second_ref.at[at], grad_w_out_hbm.at[0, at], second_sem.at[index]
+        )
+
+    def first_grad(index, carry):
+        at = pl.ds(pl.multiple_of(index * first_rows, first_rows), first_rows)
+        first_ref[at, :] = matmul(rows_ref[:, at], pre_grad_ref[...], TN).astype(jnp.bfloat16)
+        first_out(index).start()
+        return carry
+
+    def second_grad(index, carry):
+        at = pl.ds(pl.multiple_of(index * second_rows, second_rows), second_rows)
+        second_ref[at, :] = matmul(act_ref[:, at], scaled_ref[...], TN).astype(jnp.bfloat16)
+        second_out(index).start()
+        return carry
+
+    forward(0)
+    load_in.wait()
+    load_out.wait()
+    compute(0)
+    forward(1)
+    give_back(0)
+    compute(1)
+    first_count = width // first_rows
+    second_count = hidden // second_rows
+    lax.fori_loop(0, 1, first_grad, 0)
+    give_back(1)
+    lax.fori_loop(1, first_count, first_grad, 0)
+    lax.fori_loop(0, second_count, second_grad, 0)
+
+    for step in range(1, experts):
+        ret_copy(step).wait_recv()
+    summed = matmul(select_ref[...], back_ref[...], TN)
+    score_grad = (
+        summed[:, width : width + experts] + summed[:, width + experts : width + 2 * experts]
+    )
+    grad_logits = probs * (score_grad - jnp.sum(probs * score_grad, axis=-1, keepdims=True))
+    grad_logits_ref[...] = grad_logits
+    router_part = lax.dot_general(
+        grad_logits,
+        router_ref[...],
+        (NT, ((), ())),
+        precision=lax.Precision.HIGHEST,
+        preferred_element_type=jnp.float32,
+    )
+    grad_tokens_ref[...] = (summed[:, :width] + router_part).astype(jnp.bfloat16)
+
+    for step in range(1, experts):
+        go_copy(step).wait_send()
+        ret_copy(step).wait_send()
+    for step in range(experts):
+        fwd_copy(step).wait_send()
+    for part in range(2):
+        pair_copy(part).wait_send()
+    for index in range(first_count):
+        first_out(index).wait()
+    for index in range(second_count):
+        second_out(index).wait()
+
+
+def fused_body(tokens, grad_out, probs, choices, w_in, w_out, router):
+    tok_dev, width = tokens.shape
+    experts, capacity = choices.shape
+    hidden = w_in.shape[2]
+    slots = 2 * capacity // (experts * lax.axis_size("hidden"))
+    total = experts * slots
+    half_type = jnp.bfloat16
+    vmem = pl.BlockSpec(memory_space=pltpu.VMEM)
+    hbm = pl.BlockSpec(memory_space=pl.ANY)
+    dma = pltpu.SemaphoreType.DMA
+    grad_tokens, grad_logits, grad_w_in, grad_w_out = pl.pallas_call(
+        functools.partial(fused_kernel, experts, slots, 512),
+        out_shape=(
+            jax.ShapeDtypeStruct(tokens.shape, half_type),
+            jax.ShapeDtypeStruct(probs.shape, jnp.float32),
+            jax.ShapeDtypeStruct(w_in.shape, half_type),
+            jax.ShapeDtypeStruct(w_out.shape, half_type),
+        ),
+        in_specs=[vmem, vmem, vmem, vmem, vmem, hbm, hbm],
+        out_specs=(vmem, vmem, hbm, hbm),
+        scratch_shapes=[
+            pltpu.VMEM((width, hidden), half_type),
+            pltpu.VMEM((hidden, width), half_type),
+            pltpu.VMEM((total, tok_dev), half_type),
+            pltpu.VMEM((total, 2 * width + 128), half_type),
+            pltpu.VMEM((2 * total, 2 * width + 128), half_type),
+            pltpu.VMEM((2 * total, width), half_type),
+            pltpu.VMEM((2 * total, hidden), half_type),
+            pltpu.VMEM((2 * total, hidden), half_type),
+            pltpu.VMEM((2, total, width + 128), jnp.float32),
+            pltpu.VMEM((2, total // 2, width + 128), jnp.float32),
+            pltpu.VMEM((total, width + 128), half_type),
+            pltpu.VMEM((total, width + 128), half_type),
+            pltpu.VMEM((width, hidden), half_type),
+            pltpu.VMEM((hidden, width), half_type),
+            dma((2,)),
+            dma((experts,)),
+            dma((experts,)),
+            dma((experts,)),
+            dma((experts,)),
+            dma((2,)),
+            dma((2,)),
+            dma((experts,)),
+            dma((experts,)),
+            dma((width // 256,)),
+            dma((hidden // 256,)),
+        ],
+        compiler_params=pltpu.CompilerParams(
+            collective_id=0, has_side_effects=True, vmem_limit_bytes=48 * 1024 * 1024
+        ),
+        cost_estimate=pl.CostEstimate(
+            flops=20 * total * width * hidden,
+            bytes_accessed=8 * width * hidden,
+            transcendentals=2 * total * hidden,
+        ),
+    )(tokens, grad_out, probs, choices, router, w_in, w_out)
+    return (grad_tokens, grad_w_in, grad_w_out, grad_logits)
+
+
+def body(tokens, grad_out, probs, choices, w_in, w_out, router):
+    experts, capacity = choices.shape
+    owners = experts * lax.axis_size("hidden")
+    slots = 2 * capacity // owners
+    fits = (
+        lax.axis_size("hidden") == 2
+        and experts % 2 == 0
+        and slots % 16 == 0
+        and w_in.shape[0] == 1
+        and 2 * experts <= 128
+        and w_in.shape[1] % 256 == 0
+        and w_in.shape[2] % 512 == 0
+    )
+    chosen = fused_body if fits else general_body
+    return chosen(tokens, grad_out, probs, choices, w_in, w_out, router)
+
+
 def solution(mesh):
     in_specs = (
         P(("groups", "expert", "hidden"), None),

time: 130 us -> 56.1 us (0.43)
  waiting for transfers between devices: 44.6 us -> 0 us
  Pallas kernels: 0 us -> 43.5 us
  matrix products: 28.4 us -> 0 us
  blocking collectives: 24.7 us -> 0 us
  starting transfers between devices: 23 us -> 0 us
  local copies, waits for them, and re-layouts: 3.97 us -> 11.6 us
  other arithmetic: 4.23 us -> 0 us
    all_to_all x4 -> x0, waiting for transfers between devices: 44.6 us -> none  [the longest x1 27.5 us: body(): lax.all_to_all(input_part, ('expert', 'hidden'), split_axis=0, concat_axi...]
    pallas_call x0 -> x1, Pallas kernels: none -> 43.5 us  [fused_body(): pl.pallas_call(functools.partial(fused_kernel, experts, slots, 512), out_...]
    dot_general x11 -> x0, matrix products: 28.4 us -> none  [the longest x1 4.84 us: expert_pass(): lax.dot_general(scaled_grad, w_second, (((1,), (1,)), ((), ())), preferre...]
    all_to_all x1 -> x0, blocking collectives: 24.7 us -> none  [body(): lax.all_to_all(doubled(send_tokens), ('expert', 'hidden'), split_axis=0,...]
    all_to_all x4 -> x0, starting transfers between devices: 23 us -> none  [the longest x1 6.5 us: body(): lax.all_to_all(doubled(send_gates), ('expert', 'hidden'), split_axis=0, c...]
    unnamed x12 -> x14, local copies, waits for them, and re-layouts: 1.17 us -> 11.6 us
    reduce_sum x4 -> x0, other arithmetic: 3.64 us -> none  [the longest x1 1.63 us: body(): jnp.sum(back_rows.reshape(experts, hidden_count, slot_count, width), axis=1)]
    all_to_all x2 -> x0, local copies, waits for them, and re-layouts: 1.3 us -> none  [the longest x1 0.69 us: body(): lax.all_to_all(gate_part, ('expert', 'hidden'), split_axis=0, concat_axis...]
  transfers between devices with their start and end apart: 4 -> 0, of which waited for: 3 -> 0; matrix products, arithmetic and copies ran while one was open for 17% -> 0% of each run, Pallas kernels for 0% -> 0%
where the time goes in v1:
time: 56.1 us; the launch traced here: 55.7 us
  Pallas kernels  43.5 us (78%)
  local copies, waits for them, and re-layouts  11.6 us (21%)
  between operations  0.67 us (1%)
    pallas_call x1, Pallas kernels, fused_body(): pl.pallas_call(functools.partial(fused_kernel, experts, slots, 512), out_...  43.5 us
    unnamed x14, local copies, waits for them, and re-layouts  11.6 us

profile of v1, /device:TPU:19, one launch (start us, length us, event | category | flops | bytes accessed | tf_op | source)
XLA Modules:
  0.0 55.7 jit_solution(8208534014102913121)
XLA Ops:
  0.6 0.8 %copy.11.probs_ref = f32[128,8]{1,0:T(8,128)S(1)} copy(f32[128,8]{0,1:T(8,128)} %param.9) | data formatting | bytes 8192 | tf_op args[2]
  1.4 0.9 %copy.12.router_ref = f32[768,8]{1,0:T(8,128)S(1)} copy(f32[768,8]{0,1:T(8,128)} %param.13) | data formatting | bytes 49152 | tf_op args[6]
  2.3 0.0 copy-start.1
  2.3 0.9 %copy-done.1 = bf16[128,768]{1,0:T(8,128)(2,1)S(1)} copy-done((bf16[128,768]{1,0:T(8,128)(2,1)S(1)}, bf16[128,768]{1,0:T(8,128)(2,1)}, u32[]{:S(2)}) %copy-start.1) | copy-done | bytes 196632
  3.3 0.0 copy-start.2
  3.3 0.9 %copy-done.2 = bf16[128,768]{1,0:T(8,128)(2,1)S(1)} copy-done((bf16[128,768]{1,0:T(8,128)(2,1)S(1)}, bf16[128,768]{1,0:T(8,128)(2,1)}, u32[]{:S(2)}) %copy-start.2) | copy-done | bytes 196632
  4.2 0.0 copy-start.3
  4.2 0.7 %copy-done.3 = s32[8,256]{1,0:T(8,128)S(1)} copy-done((s32[8,256]{1,0:T(8,128)S(1)}, s32[8,256]{1,0:T(8,128)}, u32[]{:S(2)}) %copy-start.3) | copy-done | bytes 8216
  4.9 43.5 %shard_map.102 = (bf16[128,768]{1,0:T(8,128)(2,1)S(1)}, f32[128,8]{1,0:T(8,128)S(1)}, bf16[1,768,1536]{2,1,0:T(8,128)(2,1)S(1)}, bf16[1,1536,768]{2,1,0:T(8,128)(2,1)S(1)}) custom-call(bf16[128,768]{1,0:T(8,128)(2,1)S(1)} %copy-done.1, bf16[128,768]{1,0:T(8,128)(2,1)S(1)} %copy-done.2, f32[128,8]{1,0:T(8,128)S(1)} %copy.11.probs_ref, ...), custom_call_target="tpu_custom_call" | custom-call | flops 6039797760 | bytes 9437184 | tf_op jit(solution)/shard_map/pallas_call | solution.py:474
  48.4 0.0 copy-start
  48.4 1.4 %copy-done = bf16[1,768,1536]{2,1,0:T(8,128)(2,1)} copy-done((bf16[1,768,1536]{2,1,0:T(8,128)(2,1)}, bf16[1,768,1536]{2,1,0:T(8,128)(2,1)S(1)}, u32[]{:S(2)}) %copy-start) | copy-done | bytes 2359320
  49.8 0.7 %copy.13 = f32[128,8]{0,1:T(8,128)} copy(f32[128,8]{1,0:T(8,128)S(1)} %get-tuple-element.15) | data formatting | bytes 8192
  50.4 0.7 %copy.17 = bf16[128,768]{1,0:T(8,128)(2,1)} copy(bf16[128,768]{1,0:T(8,128)(2,1)S(1)} %get-tuple-element.20) | data formatting | bytes 393216
  51.1 3.2 %copy.18 = bf16[1,768,1536]{2,1,0:T(8,128)(2,1)} copy(bf16[1,768,1536]{2,1,0:T(8,128)(2,1)} %copy-done) | data formatting | bytes 4718592
  54.3 1.4 %copy.19 = bf16[1,1536,768]{2,1,0:T(8,128)(2,1)} copy(bf16[1,1536,768]{2,1,0:T(8,128)(2,1)S(1)} %get-tuple-element.22) | data formatting | bytes 4718592
Async XLA Ops:
  2.3 0.9 %copy-start.1 = (bf16[128,768]{1,0:T(8,128)(2,1)S(1)}, bf16[128,768]{1,0:T(8,128)(2,1)}, u32[]{:S(2)}) copy-start(bf16[128,768]{1,0:T(8,128)(2,1)} %tokens_ref.1) | copy-start | bytes 589828
  3.3 0.9 %copy-start.2 = (bf16[128,768]{1,0:T(8,128)(2,1)S(1)}, bf16[128,768]{1,0:T(8,128)(2,1)}, u32[]{:S(2)}) copy-start(bf16[128,768]{1,0:T(8,128)(2,1)} %grads_ref.1) | copy-start | bytes 589828
  4.2 0.7 %copy-start.3 = (s32[8,256]{1,0:T(8,128)S(1)}, s32[8,256]{1,0:T(8,128)}, u32[]{:S(2)}) copy-start(s32[8,256]{1,0:T(8,128)} %choices_ref.1) | copy-start | bytes 24580
  48.4 1.4 %copy-start = (bf16[1,768,1536]{2,1,0:T(8,128)(2,1)}, bf16[1,768,1536]{2,1,0:T(8,128)(2,1)S(1)}, u32[]{:S(2)}) copy-start(bf16[1,768,1536]{2,1,0:T(8,128)(2,1)S(1)} %get-tuple-element.21) | copy-start | bytes 7077892

commit v2 on v1

--- a/solution.py
+++ b/solution.py
@@ -178,17 +178,22 @@
     experts,
     slots,
     tile,
+    tokens_hbm,
+    grads_hbm,
+    probs_hbm,
+    choices_hbm,
+    router_hbm,
+    w_in_hbm,
+    w_out_hbm,
+    grad_tokens_ref,
+    grad_logits_ref,
+    first_ref,
+    second_ref,
     tokens_ref,
     grads_ref,
     probs_ref,
     choices_ref,
     router_ref,
-    w_in_hbm,
-    w_out_hbm,
-    grad_tokens_ref,
-    grad_logits_ref,
-    grad_w_in_hbm,
-    grad_w_out_hbm,
     w_in_ref,
     w_out_ref,
     select_ref,
@@ -201,9 +206,7 @@
     pair_ref,
     ret_ref,
     back_ref,
-    first_ref,
-    second_ref,
-    weight_sem,
+    load_sem,
     go_send,
     go_recv,
     fwd_send,
@@ -212,8 +215,6 @@
     pair_recv,
     ret_send,
     ret_recv,
-    first_sem,
-    second_sem,
 ):
     tok_dev, width = tokens_ref.shape
     hidden = w_in_ref.shape[1]
@@ -243,10 +244,22 @@
             barrier, inc=1, device_id={"expert": target(step)}, device_id_type=MESH
         )
     pl.semaphore_signal(barrier, inc=1, device_id=sibling, device_id_type=MESH)
-    load_in = pltpu.make_async_copy(w_in_hbm.at[0], w_in_ref, weight_sem.at[0])
-    load_out = pltpu.make_async_copy(w_out_hbm.at[0], w_out_ref, weight_sem.at[1])
-    load_in.start()
-    load_out.start()
+    loads = [
+        pltpu.make_async_copy(taken, kept, load_sem.at[index])
+        for index, (taken, kept) in enumerate(
+            (
+                (choices_hbm, choices_ref),
+                (tokens_hbm, tokens_ref),
+                (grads_hbm, grads_ref),
+                (probs_hbm, probs_ref),
+                (router_hbm, router_ref),
+                (w_in_hbm.at[0], w_in_ref),
+                (w_out_hbm.at[0], w_out_ref),
+            )
+        )
+    ]
+    for load in loads:
+        load.start()
 
     def go_copy(step):
         return pltpu.make_async_remote_copy(
@@ -288,6 +301,8 @@
             device_id_type=MESH,
         )
 
+    for load in loads[:4]:
+        load.wait()
     probs = probs_ref[...]
     probs_half = probs.astype(jnp.bfloat16)
     capacity = choices_ref.shape[1]
@@ -308,7 +323,7 @@
         chosen = select_ref[pl.ds(part * chunk, chunk), :]
         token_rows = matmul(chosen, tokens_ref[...], NN).astype(jnp.bfloat16)
         grad_rows = matmul(chosen, grads_ref[...], NN).astype(jnp.bfloat16)
-        gates = matmul(chosen, probs_half, NN)
+        gates = matmul(chosen, probs_half, NT)
         for index in range(half):
             step = part * half + index
             mine = slice(index * slots, (index + 1) * slots)
@@ -393,33 +408,19 @@
     first_rows = 256
     second_rows = 256
 
-    def first_out(index):
-        at = pl.ds(pl.multiple_of(index * first_rows, first_rows), first_rows)
-        return pltpu.make_async_copy(
-            first_ref.at[at], grad_w_in_hbm.at[0, at], first_sem.at[index]
-        )
-
-    def second_out(index):
-        at = pl.ds(pl.multiple_of(index * second_rows, second_rows), second_rows)
-        return pltpu.make_async_copy(
-            second_ref.at[at], grad_w_out_hbm.at[0, at], second_sem.at[index]
-        )
-
     def first_grad(index, carry):
         at = pl.ds(pl.multiple_of(index * first_rows, first_rows), first_rows)
-        first_ref[at, :] = matmul(rows_ref[:, at], pre_grad_ref[...], TN).astype(jnp.bfloat16)
-        first_out(index).start()
+        first_ref[0, at, :] = matmul(rows_ref[:, at], pre_grad_ref[...], TN).astype(jnp.bfloat16)
         return carry
 
     def second_grad(index, carry):
         at = pl.ds(pl.multiple_of(index * second_rows, second_rows), second_rows)
-        second_ref[at, :] = matmul(act_ref[:, at], scaled_ref[...], TN).astype(jnp.bfloat16)
-        second_out(index).start()
+        second_ref[0, at, :] = matmul(act_ref[:, at], scaled_ref[...], TN).astype(jnp.bfloat16)
         return carry
 
     forward(0)
-    load_in.wait()
-    load_out.wait()
+    for load in loads[4:]:
+        load.wait()
     compute(0)
     forward(1)
     give_back(0)
@@ -433,20 +434,19 @@
 
     for step in range(1, experts):
         ret_copy(step).wait_recv()
-    summed = matmul(select_ref[...], back_ref[...], TN)
-    score_grad = (
-        summed[:, width : width + experts] + summed[:, width + experts : width + 2 * experts]
-    )
-    grad_logits = probs * (score_grad - jnp.sum(probs * score_grad, axis=-1, keepdims=True))
+    scores = matmul(back_ref[:, width:], select_ref[...], TN)
+    score_grad = scores[:experts] + scores[experts : 2 * experts]
+    grad_logits = probs * (score_grad - jnp.sum(probs * score_grad, axis=0, keepdims=True))
     grad_logits_ref[...] = grad_logits
     router_part = lax.dot_general(
         grad_logits,
         router_ref[...],
-        (NT, ((), ())),
+        (TN, ((), ())),
         precision=lax.Precision.HIGHEST,
         preferred_element_type=jnp.float32,
     )
-    grad_tokens_ref[...] = (summed[:, :width] + router_part).astype(jnp.bfloat16)
+    moe_grad = matmul(select_ref[...], back_ref[:, :width], TN)
+    grad_tokens_ref[...] = (moe_grad + router_part).astype(jnp.bfloat16)
 
     for step in range(1, experts):
         go_copy(step).wait_send()
@@ -455,10 +455,18 @@
         fwd_copy(step).wait_send()
     for part in range(2):
         pair_copy(part).wait_send()
-    for index in range(first_count):
-        first_out(index).wait()
-    for index in range(second_count):
-        second_out(index).wait()
+
+
+def write_kernel(*refs):
+    count = len(refs) // 2
+    copies = [
+        pltpu.make_async_copy(refs[index], refs[count + index], refs[-1].at[index])
+        for index in range(count)
+    ]
+    for copy in copies:
+        copy.start()
+    for copy in copies:
+        copy.wait()
 
 
 def fused_body(tokens, grad_out, probs, choices, w_in, w_out, router):
@@ -469,19 +477,25 @@
     total = experts * slots
     half_type = jnp.bfloat16
     vmem = pl.BlockSpec(memory_space=pltpu.VMEM)
-    hbm = pl.BlockSpec(memory_space=pl.ANY)
+    hbm = pl.BlockSpec(memory_space=pltpu.HBM)
     dma = pltpu.SemaphoreType.DMA
-    grad_tokens, grad_logits, grad_w_in, grad_w_out = pl.pallas_call(
+    shapes = (
+        jax.ShapeDtypeStruct(tokens.shape, half_type),
+        jax.ShapeDtypeStruct(probs.shape[::-1], jnp.float32),
+        jax.ShapeDtypeStruct(w_in.shape, half_type),
+        jax.ShapeDtypeStruct(w_out.shape, half_type),
+    )
+    held = pl.pallas_call(
         functools.partial(fused_kernel, experts, slots, 512),
-        out_shape=(
-            jax.ShapeDtypeStruct(tokens.shape, half_type),
-            jax.ShapeDtypeStruct(probs.shape, jnp.float32),
-            jax.ShapeDtypeStruct(w_in.shape, half_type),
-            jax.ShapeDtypeStruct(w_out.shape, half_type),
-        ),
-        in_specs=[vmem, vmem, vmem, vmem, vmem, hbm, hbm],
-        out_specs=(vmem, vmem, hbm, hbm),
+        out_shape=shapes,
+        in_specs=[hbm] * 7,
+        out_specs=(vmem,) * 4,
         scratch_shapes=[
+            pltpu.VMEM(tokens.shape, half_type),
+            pltpu.VMEM(tokens.shape, half_type),
+            pltpu.VMEM(probs.shape[::-1], jnp.float32),
+            pltpu.VMEM(choices.shape, jnp.int32),
+            pltpu.VMEM(router.shape[::-1], jnp.float32),
             pltpu.VMEM((width, hidden), half_type),
             pltpu.VMEM((hidden, width), half_type),
             pltpu.VMEM((total, tok_dev), half_type),
@@ -494,9 +508,7 @@
             pltpu.VMEM((2, total // 2, width + 128), jnp.float32),
             pltpu.VMEM((total, width + 128), half_type),
             pltpu.VMEM((total, width + 128), half_type),
-            pltpu.VMEM((width, hidden), half_type),
-            pltpu.VMEM((hidden, width), half_type),
-            dma((2,)),
+            dma((7,)),
             dma((experts,)),
             dma((experts,)),
             dma((experts,)),
@@ -505,8 +517,6 @@
             dma((2,)),
             dma((experts,)),
             dma((experts,)),
-            dma((width // 256,)),
-            dma((hidden // 256,)),
         ],
         compiler_params=pltpu.CompilerParams(
             collective_id=0, has_side_effects=True, vmem_limit_bytes=48 * 1024 * 1024
@@ -516,8 +526,16 @@
             bytes_accessed=8 * width * hidden,
             transcendentals=2 * total * hidden,
         ),
-    )(tokens, grad_out, probs, choices, router, w_in, w_out)
-    return (grad_tokens, grad_w_in, grad_w_out, grad_logits)
+    )(tokens, grad_out, probs.T, choices, router.T, w_in, w_out)
+    grad_tokens, grad_logits, grad_w_in, grad_w_out = pl.pallas_call(
+        write_kernel,
+        out_shape=shapes,
+        in_specs=[pl.BlockSpec(memory_space=pl.ANY)] * 4,
+        out_specs=(hbm,) * 4,
+        scratch_shapes=[dma((4,))],
+        compiler_params=pltpu.CompilerParams(vmem_limit_bytes=1024 * 1024),
+    )(*held)
+    return (grad_tokens, grad_w_in, grad_w_out, grad_logits.T)
 
 
 def body(tokens, grad_out, probs, choices, w_in, w_out, router):

time: 56.1 us -> 50.7 us (0.904)
  local copies, waits for them, and re-layouts: 11.6 us -> 3.97 us
  Pallas kernels: 43.5 us -> 45.8 us
    unnamed x14 -> x10, local copies, waits for them, and re-layouts: 11.6 us -> 3.97 us
    pallas_call x0 -> x1, Pallas kernels: none -> 2.29 us  [fused_body(): pl.pallas_call(write_kernel, out_shape=shapes, in_specs=[pl.BlockSpec(mem...]
where the time goes in v2:
time: 50.7 us; the launch traced here: 50.4 us
  Pallas kernels  45.8 us (90%)
  local copies, waits for them, and re-layouts  3.97 us (8%)
  between operations  0.65 us (1%)
    pallas_call x1, Pallas kernels, fused_body(): pl.pallas_call(functools.partial(fused_kernel, experts, slots, 512), out_...  43.5 us
    unnamed x10, local copies, waits for them, and re-layouts  3.97 us
    pallas_call x1, Pallas kernels, fused_body(): pl.pallas_call(write_kernel, out_shape=shapes, in_specs=[pl.BlockSpec(mem...  2.29 us

profile of v2, /device:TPU:19, one launch (start us, length us, event | category | flops | bytes accessed | tf_op | source)
XLA Modules:
  0.0 50.4 jit_solution(14989372166359164983)
XLA Ops:
  0.6 0.0 copy-start
  0.6 0.9 %copy-done = bf16[128,768]{1,0:T(8,128)(2,1)S(1)} copy-done((bf16[128,768]{1,0:T(8,128)(2,1)S(1)}, bf16[128,768]{1,0:T(8,128)(2,1)}, u32[]{:S(2)}) %copy-start) | copy-done | bytes 196632
  1.6 0.0 copy-start.1
  1.6 0.9 %copy-done.1 = bf16[128,768]{1,0:T(8,128)(2,1)S(1)} copy-done((bf16[128,768]{1,0:T(8,128)(2,1)S(1)}, bf16[128,768]{1,0:T(8,128)(2,1)}, u32[]{:S(2)}) %copy-start.1) | copy-done | bytes 196632
  2.5 0.0 copy-start.2
  2.5 0.7 %copy-done.2 = f32[768,8]{0,1:T(8,128)S(1)} copy-done((f32[768,8]{0,1:T(8,128)S(1)}, f32[768,8]{0,1:T(8,128)}, u32[]{:S(2)}) %copy-start.2) | copy-done | bytes 24600
  3.2 0.0 copy-start.3
  3.2 0.7 %copy-done.3 = s32[8,256]{1,0:T(8,128)S(1)} copy-done((s32[8,256]{1,0:T(8,128)S(1)}, s32[8,256]{1,0:T(8,128)}, u32[]{:S(2)}) %copy-start.3) | copy-done | bytes 8216
  3.9 0.0 copy-start.4
  3.9 0.7 %copy-done.4 = f32[128,8]{0,1:T(8,128)S(1)} copy-done((f32[128,8]{0,1:T(8,128)S(1)}, f32[128,8]{0,1:T(8,128)}, u32[]{:S(2)}) %copy-start.4) | copy-done | bytes 4120
  4.6 43.5 %shard_map.102 = (bf16[128,768]{1,0:T(8,128)(2,1)S(1)}, f32[8,128]{1,0:T(8,128)S(1)}, bf16[1,768,1536]{2,1,0:T(8,128)(2,1)S(1)}, bf16[1,1536,768]{2,1,0:T(8,128)(2,1)S(1)}) custom-call(bf16[128,768]{1,0:T(8,128)(2,1)S(1)} %copy-done, bf16[128,768]{1,0:T(8,128)(2,1)S(1)} %copy-done.1, f32[8,128]{1,0:T(8,128)S(1)} %bitcast.4, s32[8,256]{1,0:T(8,128)S(1)} %copy-done.3, ...), custom_call_target="tpu_custom_call" | custom-call | flops 6039797760 | bytes 9437184 | tf_op jit(solution)/shard_map/pallas_call | solution.py:488
  48.1 2.3 %shard_map.103 = (bf16[128,768]{1,0:T(8,128)(2,1)}, f32[8,128]{1,0:T(8,128)}, bf16[1,768,1536]{2,1,0:T(8,128)(2,1)}, bf16[1,1536,768]{2,1,0:T(8,128)(2,1)}) custom-call(bf16[128,768]{1,0:T(8,128)(2,1)S(1)} %get-tuple-element.12.refs_0_, f32[8,128]{1,0:T(8,128)S(1)} %get-tuple-element.13.refs_1_, bf16[1,768,1536]{2,1,0:T(8,128)(2,1)S(1)} %get-tuple-element.14.refs_2_, ...), custom_call_target="tpu_custom_call" | custom-call | tf_op jit(solution)/shard_map/pallas_call | solution.py:530
Async XLA Ops:
  0.6 0.9 %copy-start = (bf16[128,768]{1,0:T(8,128)(2,1)S(1)}, bf16[128,768]{1,0:T(8,128)(2,1)}, u32[]{:S(2)}) copy-start(bf16[128,768]{1,0:T(8,128)(2,1)} %tokens_hbm.1) | copy-start | bytes 589828
  1.6 0.9 %copy-start.1 = (bf16[128,768]{1,0:T(8,128)(2,1)S(1)}, bf16[128,768]{1,0:T(8,128)(2,1)}, u32[]{:S(2)}) copy-start(bf16[128,768]{1,0:T(8,128)(2,1)} %grads_hbm.1) | copy-start | bytes 589828
  2.5 0.7 %copy-start.2 = (f32[768,8]{0,1:T(8,128)S(1)}, f32[768,8]{0,1:T(8,128)}, u32[]{:S(2)}) copy-start(f32[768,8]{0,1:T(8,128)} %param.13) | copy-start | bytes 73732
  3.2 0.7 %copy-start.3 = (s32[8,256]{1,0:T(8,128)S(1)}, s32[8,256]{1,0:T(8,128)}, u32[]{:S(2)}) copy-start(s32[8,256]{1,0:T(8,128)} %choices_hbm.1) | copy-start | bytes 24580
  3.9 0.7 %copy-start.4 = (f32[128,8]{0,1:T(8,128)S(1)}, f32[128,8]{0,1:T(8,128)}, u32[]{:S(2)}) copy-start(f32[128,8]{0,1:T(8,128)} %param.9) | copy-start | bytes 12292

commit v3 on v2

--- a/solution.py
+++ b/solution.py
@@ -178,22 +178,14 @@
     experts,
     slots,
     tile,
-    tokens_hbm,
-    grads_hbm,
-    probs_hbm,
-    choices_hbm,
-    router_hbm,
+    tokens_ref,
+    table_ref,
     w_in_hbm,
     w_out_hbm,
     grad_tokens_ref,
     grad_logits_ref,
     first_ref,
     second_ref,
-    tokens_ref,
-    grads_ref,
-    probs_ref,
-    choices_ref,
-    router_ref,
     w_in_ref,
     w_out_ref,
     select_ref,
@@ -216,7 +208,9 @@
     ret_send,
     ret_recv,
 ):
-    tok_dev, width = tokens_ref.shape
+    tok_dev = tokens_ref.shape[0]
+    width = w_in_ref.shape[0]
+    capacity = table_ref.shape[1] - tok_dev - width
     hidden = w_in_ref.shape[1]
     half = experts // 2
     chunk = half * slots
@@ -234,8 +228,14 @@
         where = side if step < half else 1 - side
         return where * half + (place + 2 * half - step) % half
 
+    parts = ((0, half), (half, half // 2), (half + half // 2, half - half // 2))
+
+    def place_of(step):
+        return [part for part in parts if part[0] <= step < sum(part)][0]
+
     def direct_row(step):
-        return (step // half) * 2 * chunk + (step % half) * slots
+        start, count = place_of(step)
+        return (step + start) * slots
 
     sibling = {"hidden": 1 - core}
     barrier = pltpu.get_barrier_semaphore()
@@ -248,11 +248,6 @@
         pltpu.make_async_copy(taken, kept, load_sem.at[index])
         for index, (taken, kept) in enumerate(
             (
-                (choices_hbm, choices_ref),
-                (tokens_hbm, tokens_ref),
-                (grads_hbm, grads_ref),
-                (probs_hbm, probs_ref),
-                (router_hbm, router_ref),
                 (w_in_hbm.at[0], w_in_ref),
                 (w_out_hbm.at[0], w_out_ref),
             )
@@ -274,7 +269,7 @@
     def fwd_copy(step):
         return pltpu.make_async_remote_copy(
             src_ref=rows_ref.at[pl.ds(direct_row(step), slots)],
-            dst_ref=rows_ref.at[pl.ds(direct_row(step) + chunk, slots)],
+            dst_ref=rows_ref.at[pl.ds(direct_row(step) + place_of(step)[1] * slots, slots)],
             send_sem=fwd_send.at[step],
             recv_sem=fwd_recv.at[step],
             device_id=sibling,
@@ -282,9 +277,10 @@
         )
 
     def pair_copy(part):
+        start, count = parts[part]
         return pltpu.make_async_remote_copy(
-            src_ref=part_ref.at[part, pl.ds(chunk, chunk)],
-            dst_ref=pair_ref.at[part],
+            src_ref=part_ref.at[pl.ds((2 * start + count) * slots, count * slots)],
+            dst_ref=pair_ref.at[pl.ds(start * slots, count * slots)],
             send_sem=pair_send.at[part],
             recv_sem=pair_recv.at[part],
             device_id=sibling,
@@ -301,28 +297,26 @@
             device_id_type=MESH,
         )
 
-    for load in loads[:4]:
-        load.wait()
-    probs = probs_ref[...]
+    probs = table_ref[:, :tok_dev]
     probs_half = probs.astype(jnp.bfloat16)
-    capacity = choices_ref.shape[1]
     rank_gap = lax.broadcasted_iota(jnp.int32, (slots, capacity), 1) - lax.broadcasted_iota(
         jnp.int32, (slots, capacity), 0
     )
     rank_gap = rank_gap.astype(jnp.float32)
     token_id = lax.broadcasted_iota(jnp.int32, (tok_dev, capacity), 0) + base
+    token_id = token_id.astype(jnp.float32)
+    first_token = token_id[:1, :]
     column = lax.broadcasted_iota(jnp.int32, (slots, experts), 1)
 
     def select(part):
         for step in range(part * half, (part + 1) * half):
-            row = choices_ref[pl.ds(target(step), 1), :]
-            before = jnp.sum(jnp.where(row < base, 1.0, 0.0), axis=1, keepdims=True)
+            row = table_ref[pl.ds(target(step), 1), tok_dev + width :]
+            before = jnp.sum(jnp.where(row < first_token, 1.0, 0.0), axis=1, keepdims=True)
             pick = jnp.where(rank_gap == before, 1.0, 0.0).astype(jnp.bfloat16)
             equal = jnp.where(token_id == row, 1.0, 0.0).astype(jnp.bfloat16)
             select_ref[pl.ds(step * slots, slots), :] = matmul(pick, equal, NT).astype(jnp.bfloat16)
         chosen = select_ref[pl.ds(part * chunk, chunk), :]
-        token_rows = matmul(chosen, tokens_ref[...], NN).astype(jnp.bfloat16)
-        grad_rows = matmul(chosen, grads_ref[...], NN).astype(jnp.bfloat16)
+        both_rows = matmul(chosen, tokens_ref[...], NN).astype(jnp.bfloat16)
         gates = matmul(chosen, probs_half, NT)
         for index in range(half):
             step = part * half + index
@@ -333,34 +327,36 @@
             gate = jnp.broadcast_to(gate, (slots, 128)).astype(jnp.bfloat16)
             ref = rows_ref if step == 0 else send_ref
             at = pl.ds(step * slots, slots)
-            ref[at, :width] = token_rows[mine]
-            ref[at, width : 2 * width] = grad_rows[mine]
+            ref[at, : 2 * width] = both_rows[mine]
             ref[at, 2 * width :] = gate
 
     select(1)
     pl.semaphore_wait(barrier, experts)
-    for step in range(half, experts):
+    for step in range(half, sum(parts[1])):
         go_copy(step).start()
     select(0)
     for step in range(1, half):
         go_copy(step).start()
+    for step in range(parts[2][0], experts):
+        go_copy(step).start()
 
     def forward(part):
-        for step in range(part * half, (part + 1) * half):
+        for step in range(parts[part][0], sum(parts[part])):
             if step:
                 go_copy(step).wait_recv()
             fwd_copy(step).start()
 
     def compute(part):
-        for step in range(part * half, (part + 1) * half):
+        start, count = parts[part]
+        for step in range(start, start + count):
             fwd_copy(step).wait_recv()
-        rows = pl.ds(part * 2 * chunk, 2 * chunk)
+        rows = pl.ds(2 * start * slots, 2 * count * slots)
         gate = rows_ref[rows, 2 * width :].astype(jnp.float32)
         wide_gate = jnp.concatenate([gate] * (width // 128), axis=1)
         scaled_ref[rows, :] = (
             wide_gate * rows_ref[rows, width : 2 * width].astype(jnp.float32)
         ).astype(jnp.bfloat16)
-        part_ref[part] = jnp.zeros(part_ref.shape[1:], jnp.float32)
+        part_ref[rows, :] = jnp.zeros((2 * count * slots, width + 128), jnp.float32)
 
         def step_tile(index, carry):
             at = pl.ds(pl.multiple_of(index * tile, tile), tile)
@@ -375,29 +371,30 @@
             gate_tile = jnp.concatenate([gate] * (tile // 128), axis=1)
             pre_grad = (gate_tile * raw_grad * gelu_slope).astype(jnp.bfloat16)
             pre_grad_ref[rows, at] = pre_grad
-            part_ref[part, :, :width] += matmul(pre_grad, w_first, NT)
+            part_ref[rows, :width] += matmul(pre_grad, w_first, NT)
             total = product[:, :128]
             for lane in range(128, tile, 128):
                 total = total + product[:, lane : lane + 128]
-            part_ref[part, :, width:] += total
+            part_ref[rows, width:] += total
             return carry
 
         lax.fori_loop(0, hidden // tile, step_tile, 0)
         pair_copy(part).start()
 
-    lane = lax.broadcasted_iota(jnp.int32, (chunk, 128), 1)
-
     def give_back(part):
         pair_copy(part).wait_recv()
-        total = part_ref[part, :chunk, :] + pair_ref[part]
+        start, count = parts[part]
+        lane = lax.broadcasted_iota(jnp.int32, (count * slots, 128), 1)
+        own = part_ref[pl.ds(2 * start * slots, count * slots), :]
+        total = own + pair_ref[pl.ds(start * slots, count * slots), :]
         gate_grad = jnp.sum(total[:, width:], axis=1, keepdims=True)
         high = gate_grad.astype(jnp.bfloat16).astype(jnp.float32)
         low = gate_grad - high
         coded = jnp.where(lane == me, high, jnp.where(lane == me + experts, low, 0.0))
         values = total[:, :width].astype(jnp.bfloat16)
         coded = coded.astype(jnp.bfloat16)
-        for index in range(half):
-            step = part * half + index
+        for index in range(count):
+            step = start + index
             mine = slice(index * slots, (index + 1) * slots)
             ref = ret_ref if step else back_ref
             ref[pl.ds(step * slots, slots), :width] = values[mine]
@@ -418,42 +415,51 @@
         second_ref[0, at, :] = matmul(act_ref[:, at], scaled_ref[...], TN).astype(jnp.bfloat16)
         return carry
 
+    first_count = width // first_rows
+    second_count = hidden // second_rows
     forward(0)
-    for load in loads[4:]:
+    for load in loads:
         load.wait()
     compute(0)
     forward(1)
     give_back(0)
     compute(1)
-    first_count = width // first_rows
-    second_count = hidden // second_rows
+    forward(2)
+    give_back(1)
+    compute(2)
     lax.fori_loop(0, 1, first_grad, 0)
-    give_back(1)
+    give_back(2)
     lax.fori_loop(1, first_count, first_grad, 0)
     lax.fori_loop(0, second_count, second_grad, 0)
 
-    for step in range(1, experts):
-        ret_copy(step).wait_recv()
-    scores = matmul(back_ref[:, width:], select_ref[...], TN)
+    def collect(start, stop):
+        for step in range(max(start, 1), stop):
+            ret_copy(step).wait_recv()
+        rows = pl.ds(start * slots, (stop - start) * slots)
+        scores = matmul(back_ref[rows, width:], select_ref[rows, :], TN)
+        return matmul(select_ref[rows, :], back_ref[rows, :width], TN), scores
+
+    early_grad, early_scores = collect(0, half)
+    late_grad, late_scores = collect(half, experts)
+    scores = early_scores + late_scores
     score_grad = scores[:experts] + scores[experts : 2 * experts]
     grad_logits = probs * (score_grad - jnp.sum(probs * score_grad, axis=0, keepdims=True))
     grad_logits_ref[...] = grad_logits
     router_part = lax.dot_general(
         grad_logits,
-        router_ref[...],
+        table_ref[:, tok_dev : tok_dev + width],
         (TN, ((), ())),
         precision=lax.Precision.HIGHEST,
         preferred_element_type=jnp.float32,
     )
-    moe_grad = matmul(select_ref[...], back_ref[:, :width], TN)
-    grad_tokens_ref[...] = (moe_grad + router_part).astype(jnp.bfloat16)
+    grad_tokens_ref[...] = (early_grad + late_grad + router_part).astype(jnp.bfloat16)
 
     for step in range(1, experts):
         go_copy(step).wait_send()
         ret_copy(step).wait_send()
     for step in range(experts):
         fwd_copy(step).wait_send()
-    for part in range(2):
+    for part in range(len(parts)):
         pair_copy(part).wait_send()
 
 
@@ -485,17 +491,14 @@
         jax.ShapeDtypeStruct(w_in.shape, half_type),
         jax.ShapeDtypeStruct(w_out.shape, half_type),
     )
+    stacked = jnp.concatenate([tokens, grad_out], axis=1)
+    table = jnp.concatenate([probs.T, router.T, choices.astype(jnp.float32)], axis=1)
     held = pl.pallas_call(
         functools.partial(fused_kernel, experts, slots, 512),
         out_shape=shapes,
-        in_specs=[hbm] * 7,
+        in_specs=[vmem, vmem, hbm, hbm],
         out_specs=(vmem,) * 4,
         scratch_shapes=[
-            pltpu.VMEM(tokens.shape, half_type),
-            pltpu.VMEM(tokens.shape, half_type),
-            pltpu.VMEM(probs.shape[::-1], jnp.float32),
-            pltpu.VMEM(choices.shape, jnp.int32),
-            pltpu.VMEM(router.shape[::-1], jnp.float32),
             pltpu.VMEM((width, hidden), half_type),
             pltpu.VMEM((hidden, width), half_type),
             pltpu.VMEM((total, tok_dev), half_type),
@@ -504,17 +507,17 @@
             pltpu.VMEM((2 * total, width), half_type),
             pltpu.VMEM((2 * total, hidden), half_type),
             pltpu.VMEM((2 * total, hidden), half_type),
-            pltpu.VMEM((2, total, width + 128), jnp.float32),
-            pltpu.VMEM((2, total // 2, width + 128), jnp.float32),
+            pltpu.VMEM((2 * total, width + 128), jnp.float32),
+            pltpu.VMEM((total, width + 128), jnp.float32),
             pltpu.VMEM((total, width + 128), half_type),
             pltpu.VMEM((total, width + 128), half_type),
-            dma((7,)),
+            dma((2,)),
             dma((experts,)),
             dma((experts,)),
             dma((experts,)),
             dma((experts,)),
-            dma((2,)),
-            dma((2,)),
+            dma((3,)),
+            dma((3,)),
             dma((experts,)),
             dma((experts,)),
         ],
@@ -526,7 +529,7 @@
             bytes_accessed=8 * width * hidden,
             transcendentals=2 * total * hidden,
         ),
-    )(tokens, grad_out, probs.T, choices, router.T, w_in, w_out)
+    )(stacked, table, w_in, w_out)
     grad_tokens, grad_logits, grad_w_in, grad_w_out = pl.pallas_call(
         write_kernel,
         out_shape=shapes,
@@ -544,8 +547,9 @@
     slots = 2 * capacity // owners
     fits = (
         lax.axis_size("hidden") == 2
-        and experts % 2 == 0
+        and experts % 4 == 0
         and slots % 16 == 0
+        and tokens.shape[0] % 128 == 0
         and w_in.shape[0] == 1
         and 2 * experts <= 128
         and w_in.shape[1] % 256 == 0

time: 50.7 us -> 46 us (0.907)
  local copies, waits for them, and re-layouts: 3.97 us -> 0 us
  Pallas kernels: 45.8 us -> 42.6 us
  other arithmetic: 0 us -> 2.49 us
    unnamed x10 -> x0, local copies, waits for them, and re-layouts: 3.97 us -> none
    pallas_call x1, Pallas kernels: 43.5 us -> 40.4 us  [fused_body(): pl.pallas_call(functools.partial(fused_kernel, experts, slots, 512), out_...]
    concatenate x0 -> x2, other arithmetic: none -> 1.79 us  [the longest x1 1.05 us: fused_body(): stacked = jnp.concatenate([tokens, grad_out], axis=1)]
    convert_element_type x0 -> x1, other arithmetic: none -> 0.7 us  [fused_body(): choices.astype(jnp.float32)]
where the time goes in v3:
time: 46 us; the launch traced here: 45.8 us
  Pallas kernels  42.6 us (93%)
  other arithmetic  2.49 us (5%)
  between operations  0.64 us (1%)
    pallas_call x1, Pallas kernels, fused_body(): pl.pallas_call(functools.partial(fused_kernel, experts, slots, 512), out_...  40.4 us
    pallas_call x1, Pallas kernels, fused_body(): pl.pallas_call(write_kernel, out_shape=shapes, in_specs=[pl.BlockSpec(mem...  2.29 us
    concatenate x1, other arithmetic, fused_body(): stacked = jnp.concatenate([tokens, grad_out], axis=1)  1.05 us

profile of v3, /device:TPU:19, one launch (start us, length us, event | category | flops | bytes accessed | tf_op | source)
XLA Modules:
  0.0 45.8 jit_solution(312321913080822660)
XLA Ops:
  0.6 0.7 %convert_element_type.3 = f32[8,256]{1,0:T(8,128)S(1)} convert(s32[8,256]{1,0:T(8,128)} %param.10) | non-fusion elementwise | flops 2048 | bytes 16384 | tf_op jit(solution)/shard_map/convert_element_type | solution.py:495
  1.3 0.7 %pad_maximum_fusion.1.table_ref = f32[8,1152]{1,0:T(8,128)S(1)} fusion(f32[8,256]{1,0:T(8,128)S(1)} %convert_element_type.3, f32[8,768]{1,0:T(8,128)} %bitcast.3, f32[8,128]{1,0:T(8,128)} %bitcast.4), kind=kLoop, calls=%fused_computation.1 | loop fusion | flops 18432 | bytes 73728 | tf_op jit(solution)/shard_map/concatenate | solution.py:495
  2.1 1.0 %pad_maximum_fusion.tokens_ref = bf16[128,1536]{1,0:T(8,128)(2,1)S(1)} fusion(bf16[128,768]{1,0:T(8,128)(2,1)} %param.8, bf16[128,768]{1,0:T(8,128)(2,1)} %param.7), kind=kLoop, calls=%fused_computation | loop fusion | flops 786432 | bytes 786432 | tf_op jit(solution)/shard_map/concatenate | solution.py:494
  3.1 40.4 %shard_map.102 = (bf16[128,768]{1,0:T(8,128)(2,1)S(1)}, f32[8,128]{1,0:T(8,128)S(1)}, bf16[1,768,1536]{2,1,0:T(8,128)(2,1)S(1)}, bf16[1,1536,768]{2,1,0:T(8,128)(2,1)S(1)}) custom-call(bf16[128,1536]{1,0:T(8,128)(2,1)S(1)} %pad_maximum_fusion.tokens_ref, f32[8,1152]{1,0:T(8,128)S(1)} %pad_maximum_fusion.1.table_ref, bf16[1,768,1536]{2,1,0:T(8,128)(2,1)} %w_in_hbm.1, ...), custom_call_target="tpu_custom_call" | custom-call | flops 6039797760 | bytes 9437184 | tf_op jit(solution)/shard_map/pallas_call | solution.py:496
  43.5 2.3 %shard_map.103 = (bf16[128,768]{1,0:T(8,128)(2,1)}, f32[8,128]{1,0:T(8,128)}, bf16[1,768,1536]{2,1,0:T(8,128)(2,1)}, bf16[1,1536,768]{2,1,0:T(8,128)(2,1)}) custom-call(bf16[128,768]{1,0:T(8,128)(2,1)S(1)} %get-tuple-element.12.refs_0_, f32[8,128]{1,0:T(8,128)S(1)} %get-tuple-element.13.refs_1_, bf16[1,768,1536]{2,1,0:T(8,128)(2,1)S(1)} %get-tuple-element.14.refs_2_, ...), custom_call_target="tpu_custom_call" | custom-call | tf_op jit(solution)/shard_map/pallas_call | solution.py:533

commit v4 on v3

--- a/solution.py
+++ b/solution.py
@@ -188,6 +188,8 @@
     second_ref,
     w_in_ref,
     w_out_ref,
+    w_in_t_ref,
+    w_out_t_ref,
     select_ref,
     send_ref,
     rows_ref,
@@ -198,6 +200,10 @@
     pair_ref,
     ret_ref,
     back_ref,
+    gate_out_ref,
+    gate_in_ref,
+    slope_out_ref,
+    slope_in_ref,
     load_sem,
     go_send,
     go_recv,
@@ -207,6 +213,12 @@
     pair_recv,
     ret_send,
     ret_recv,
+    gate_send,
+    gate_recv,
+    gate_fwd_send,
+    gate_fwd_recv,
+    slope_send,
+    slope_recv,
 ):
     tok_dev = tokens_ref.shape[0]
     width = w_in_ref.shape[0]
@@ -276,6 +288,37 @@
             device_id_type=MESH,
         )
 
+    def gate_copy(step):
+        return pltpu.make_async_remote_copy(
+            src_ref=gate_out_ref.at[step],
+            dst_ref=gate_in_ref.at[direct_row(step) // slots],
+            send_sem=gate_send.at[step],
+            recv_sem=gate_recv.at[step],
+            device_id={"expert": target(step)},
+            device_id_type=MESH,
+        )
+
+    def gate_fwd_copy(step):
+        row = direct_row(step) // slots
+        return pltpu.make_async_remote_copy(
+            src_ref=gate_in_ref.at[row],
+            dst_ref=gate_in_ref.at[row + place_of(step)[1]],
+            send_sem=gate_fwd_send.at[step],
+            recv_sem=gate_fwd_recv.at[step],
+            device_id=sibling,
+            device_id_type=MESH,
+        )
+
+    def slope_copy(step):
+        return pltpu.make_async_remote_copy(
+            src_ref=slope_out_ref.at[step],
+            dst_ref=slope_in_ref.at[step],
+            send_sem=slope_send.at[step],
+            recv_sem=slope_recv.at[step],
+            device_id={"expert": source(step)},
+            device_id_type=MESH,
+        )
+
     def pair_copy(part):
         start, count = parts[part]
         return pltpu.make_async_remote_copy(
@@ -306,7 +349,10 @@
     token_id = lax.broadcasted_iota(jnp.int32, (tok_dev, capacity), 0) + base
     token_id = token_id.astype(jnp.float32)
     first_token = token_id[:1, :]
-    column = lax.broadcasted_iota(jnp.int32, (slots, experts), 1)
+    expert_row = lax.broadcasted_iota(jnp.int32, (experts, chunk), 0)
+    slot_gap = lax.broadcasted_iota(jnp.int32, (slots, chunk), 1) - lax.broadcasted_iota(
+        jnp.int32, (slots, chunk), 0
+    )
 
     def select(part):
         for step in range(part * half, (part + 1) * half):
@@ -317,41 +363,54 @@
             select_ref[pl.ds(step * slots, slots), :] = matmul(pick, equal, NT).astype(jnp.bfloat16)
         chosen = select_ref[pl.ds(part * chunk, chunk), :]
         both_rows = matmul(chosen, tokens_ref[...], NN).astype(jnp.bfloat16)
-        gates = matmul(chosen, probs_half, NT)
+        gates = matmul(probs_half, chosen, NT)
         for index in range(half):
             step = part * half + index
             mine = slice(index * slots, (index + 1) * slots)
             gate = jnp.sum(
-                jnp.where(column == target(step), gates[mine], 0.0), axis=1, keepdims=True
+                jnp.where(expert_row == target(step), gates, 0.0), axis=0, keepdims=True
             )
-            gate = jnp.broadcast_to(gate, (slots, 128)).astype(jnp.bfloat16)
+            gate_ref = gate_out_ref if step else gate_in_ref
+            gate_ref[step] = gate
             ref = rows_ref if step == 0 else send_ref
             at = pl.ds(step * slots, slots)
-            ref[at, : 2 * width] = both_rows[mine]
-            ref[at, 2 * width :] = gate
+            ref[at, :] = both_rows[mine]
 
     select(1)
     pl.semaphore_wait(barrier, experts)
     for step in range(half, sum(parts[1])):
         go_copy(step).start()
+        gate_copy(step).start()
     select(0)
     for step in range(1, half):
         go_copy(step).start()
+        gate_copy(step).start()
     for step in range(parts[2][0], experts):
         go_copy(step).start()
+        gate_copy(step).start()
 
     def forward(part):
         for step in range(parts[part][0], sum(parts[part])):
             if step:
                 go_copy(step).wait_recv()
+                gate_copy(step).wait_recv()
             fwd_copy(step).start()
+            gate_fwd_copy(step).start()
 
     def compute(part):
         start, count = parts[part]
         for step in range(start, start + count):
             fwd_copy(step).wait_recv()
+            gate_fwd_copy(step).wait_recv()
         rows = pl.ds(2 * start * slots, 2 * count * slots)
-        gate = rows_ref[rows, 2 * width :].astype(jnp.float32)
+        blocks = []
+        for index in range(2 * count):
+            shift = ((start + index % count) % half) * slots
+            row = jnp.broadcast_to(gate_in_ref[2 * start + index], (slots, chunk))
+            blocks.append(
+                jnp.sum(jnp.where(slot_gap == shift, row, 0.0), axis=1, keepdims=True)
+            )
+        gate = jnp.broadcast_to(jnp.concatenate(blocks, axis=0), (2 * count * slots, 128))
         wide_gate = jnp.concatenate([gate] * (width // 128), axis=1)
         scaled_ref[rows, :] = (
             wide_gate * rows_ref[rows, width : 2 * width].astype(jnp.float32)
@@ -361,9 +420,9 @@
         def step_tile(index, carry):
             at = pl.ds(pl.multiple_of(index * tile, tile), tile)
             w_first = w_in_ref[:, at]
-            w_second = w_out_ref[at, :]
+            w_second = w_out_t_ref[:, at]
             pre_act = matmul(rows_ref[rows, :width], w_first, NN)
-            raw_grad = matmul(rows_ref[rows, width : 2 * width], w_second, NT)
+            raw_grad = matmul(rows_ref[rows, width : 2 * width], w_second, NN)
             gelu_value, gelu_slope = gelu_parts(pre_act)
             act = gelu_value.astype(jnp.bfloat16)
             act_ref[rows, at] = act
@@ -371,7 +430,7 @@
             gate_tile = jnp.concatenate([gate] * (tile // 128), axis=1)
             pre_grad = (gate_tile * raw_grad * gelu_slope).astype(jnp.bfloat16)
             pre_grad_ref[rows, at] = pre_grad
-            part_ref[rows, :width] += matmul(pre_grad, w_first, NT)
+            part_ref[rows, :width] += matmul(pre_grad, w_in_t_ref[at, :], NN)
             total = product[:, :128]
             for lane in range(128, tile, 128):
                 total = total + product[:, lane : lane + 128]
@@ -384,23 +443,23 @@
     def give_back(part):
         pair_copy(part).wait_recv()
         start, count = parts[part]
-        lane = lax.broadcasted_iota(jnp.int32, (count * slots, 128), 1)
         own = part_ref[pl.ds(2 * start * slots, count * slots), :]
         total = own + pair_ref[pl.ds(start * slots, count * slots), :]
         gate_grad = jnp.sum(total[:, width:], axis=1, keepdims=True)
-        high = gate_grad.astype(jnp.bfloat16).astype(jnp.float32)
-        low = gate_grad - high
-        coded = jnp.where(lane == me, high, jnp.where(lane == me + experts, low, 0.0))
         values = total[:, :width].astype(jnp.bfloat16)
-        coded = coded.astype(jnp.bfloat16)
         for index in range(count):
             step = start + index
             mine = slice(index * slots, (index + 1) * slots)
             ref = ret_ref if step else back_ref
-            ref[pl.ds(step * slots, slots), :width] = values[mine]
-            ref[pl.ds(step * slots, slots), width:] = coded[mine]
+            ref[pl.ds(step * slots, slots), :] = values[mine]
+            spread = jnp.broadcast_to(gate_grad[mine], (slots, chunk))
+            slope_ref = slope_out_ref if step else slope_in_ref
+            slope_ref[step] = jnp.sum(
+                jnp.where(slot_gap == (step % half) * slots, spread, 0.0), axis=0, keepdims=True
+            )
             if step:
                 ret_copy(step).start()
+                slope_copy(step).start()
 
     first_rows = 256
     second_rows = 256
@@ -417,9 +476,17 @@
 
     first_count = width // first_rows
     second_count = hidden // second_rows
-    forward(0)
     for load in loads:
         load.wait()
+
+    def turn(index, carry):
+        at = pl.ds(pl.multiple_of(index * 256, 256), 256)
+        w_in_t_ref[at, :] = w_in_ref[:, at].T
+        w_out_t_ref[:, at] = w_out_ref[at, :].T
+        return carry
+
+    lax.fori_loop(0, hidden // 256, turn, 0)
+    forward(0)
     compute(0)
     forward(1)
     give_back(0)
@@ -435,14 +502,20 @@
     def collect(start, stop):
         for step in range(max(start, 1), stop):
             ret_copy(step).wait_recv()
+            slope_copy(step).wait_recv()
         rows = pl.ds(start * slots, (stop - start) * slots)
-        scores = matmul(back_ref[rows, width:], select_ref[rows, :], TN)
-        return matmul(select_ref[rows, :], back_ref[rows, :width], TN), scores
+        coded = jnp.zeros((experts, chunk), jnp.float32)
+        for step in range(start, stop):
+            coded += jnp.where(expert_row == target(step), slope_in_ref[step], 0.0)
+        high = coded.astype(jnp.bfloat16)
+        low = (coded - high.astype(jnp.float32)).astype(jnp.bfloat16)
+        chosen = select_ref[rows, :]
+        scores = matmul(high, chosen, NN) + matmul(low, chosen, NN)
+        return matmul(chosen, back_ref[rows, :], TN), scores
 
     early_grad, early_scores = collect(0, half)
     late_grad, late_scores = collect(half, experts)
-    scores = early_scores + late_scores
-    score_grad = scores[:experts] + scores[experts : 2 * experts]
+    score_grad = early_scores + late_scores
     grad_logits = probs * (score_grad - jnp.sum(probs * score_grad, axis=0, keepdims=True))
     grad_logits_ref[...] = grad_logits
     router_part = lax.dot_general(
@@ -456,9 +529,12 @@
 
     for step in range(1, experts):
         go_copy(step).wait_send()
+        gate_copy(step).wait_send()
         ret_copy(step).wait_send()
+        slope_copy(step).wait_send()
     for step in range(experts):
         fwd_copy(step).wait_send()
+        gate_fwd_copy(step).wait_send()
     for part in range(len(parts)):
         pair_copy(part).wait_send()
 
@@ -501,16 +577,22 @@
         scratch_shapes=[
             pltpu.VMEM((width, hidden), half_type),
             pltpu.VMEM((hidden, width), half_type),
+            pltpu.VMEM((hidden, width), half_type),
+            pltpu.VMEM((width, hidden), half_type),
             pltpu.VMEM((total, tok_dev), half_type),
-            pltpu.VMEM((total, 2 * width + 128), half_type),
-            pltpu.VMEM((2 * total, 2 * width + 128), half_type),
+            pltpu.VMEM((total, 2 * width), half_type),
+            pltpu.VMEM((2 * total, 2 * width), half_type),
             pltpu.VMEM((2 * total, width), half_type),
             pltpu.VMEM((2 * total, hidden), half_type),
             pltpu.VMEM((2 * total, hidden), half_type),
             pltpu.VMEM((2 * total, width + 128), jnp.float32),
             pltpu.VMEM((total, width + 128), jnp.float32),
-            pltpu.VMEM((total, width + 128), half_type),
-            pltpu.VMEM((total, width + 128), half_type),
+            pltpu.VMEM((total, width), half_type),
+            pltpu.VMEM((total, width), half_type),
+            pltpu.VMEM((experts, 1, 128), jnp.float32),
+            pltpu.VMEM((2 * experts, 1, 128), jnp.float32),
+            pltpu.VMEM((experts, 1, 128), jnp.float32),
+            pltpu.VMEM((experts, 1, 128), jnp.float32),
             dma((2,)),
             dma((experts,)),
             dma((experts,)),
@@ -520,7 +602,8 @@
             dma((3,)),
             dma((experts,)),
             dma((experts,)),
-        ],
+        ]
+        + [dma((experts,))] * 6,
         compiler_params=pltpu.CompilerParams(
             collective_id=0, has_side_effects=True, vmem_limit_bytes=48 * 1024 * 1024
         ),
@@ -550,6 +633,7 @@
         and experts % 4 == 0
         and slots % 16 == 0
         and tokens.shape[0] % 128 == 0
+        and experts * slots == 256
         and w_in.shape[0] == 1
         and 2 * experts <= 128
         and w_in.shape[1] % 256 == 0

time: 46 us -> 44.1 us (0.959)
  Pallas kernels: 42.6 us -> 40.7 us
    pallas_call x1, Pallas kernels: 40.4 us -> 38.4 us  [fused_body(): pl.pallas_call(functools.partial(fused_kernel, experts, slots, 512), out_...]
where the time goes in v4:
time: 44.1 us; the launch traced here: 43.9 us
  Pallas kernels  40.7 us (92%)
  other arithmetic  2.49 us (6%)
  between operations  0.64 us (1%)
    pallas_call x1, Pallas kernels, fused_body(): pl.pallas_call(functools.partial(fused_kernel, experts, slots, 512), out_...  38.4 us
    pallas_call x1, Pallas kernels, fused_body(): pl.pallas_call(write_kernel, out_shape=shapes, in_specs=[pl.BlockSpec(mem...  2.29 us
    concatenate x1, other arithmetic, fused_body(): stacked = jnp.concatenate([tokens, grad_out], axis=1)  1.05 us

profile of v4, /device:TPU:19, one launch (start us, length us, event | category | flops | bytes accessed | tf_op | source)
XLA Modules:
  0.0 43.9 jit_solution(16564728336517321861)
XLA Ops:
  0.6 0.7 %convert_element_type.3 = f32[8,256]{1,0:T(8,128)S(1)} convert(s32[8,256]{1,0:T(8,128)} %param.10) | non-fusion elementwise | flops 2048 | bytes 16384 | tf_op jit(solution)/shard_map/convert_element_type | solution.py:571
  1.3 0.7 %pad_maximum_fusion.1.table_ref = f32[8,1152]{1,0:T(8,128)S(1)} fusion(f32[8,256]{1,0:T(8,128)S(1)} %convert_element_type.3, f32[8,768]{1,0:T(8,128)} %bitcast.3, f32[8,128]{1,0:T(8,128)} %bitcast.4), kind=kLoop, calls=%fused_computation.1 | loop fusion | flops 18432 | bytes 73728 | tf_op jit(solution)/shard_map/concatenate | solution.py:571
  2.1 1.0 %pad_maximum_fusion.tokens_ref = bf16[128,1536]{1,0:T(8,128)(2,1)S(1)} fusion(bf16[128,768]{1,0:T(8,128)(2,1)} %param.8, bf16[128,768]{1,0:T(8,128)(2,1)} %param.7), kind=kLoop, calls=%fused_computation | loop fusion | flops 786432 | bytes 786432 | tf_op jit(solution)/shard_map/concatenate | solution.py:570
  3.1 38.4 %shard_map.102 = (bf16[128,768]{1,0:T(8,128)(2,1)S(1)}, f32[8,128]{1,0:T(8,128)S(1)}, bf16[1,768,1536]{2,1,0:T(8,128)(2,1)S(1)}, bf16[1,1536,768]{2,1,0:T(8,128)(2,1)S(1)}) custom-call(bf16[128,1536]{1,0:T(8,128)(2,1)S(1)} %pad_maximum_fusion.tokens_ref, f32[8,1152]{1,0:T(8,128)S(1)} %pad_maximum_fusion.1.table_ref, bf16[1,768,1536]{2,1,0:T(8,128)(2,1)} %w_in_hbm.1, ...), custom_call_target="tpu_custom_call" | custom-call | flops 6039797760 | bytes 9437184 | tf_op jit(solution)/shard_map/pallas_call | solution.py:572
  41.6 2.3 %shard_map.103 = (bf16[128,768]{1,0:T(8,128)(2,1)}, f32[8,128]{1,0:T(8,128)}, bf16[1,768,1536]{2,1,0:T(8,128)(2,1)}, bf16[1,1536,768]{2,1,0:T(8,128)(2,1)}) custom-call(bf16[128,768]{1,0:T(8,128)(2,1)S(1)} %get-tuple-element.12.refs_0_, f32[8,128]{1,0:T(8,128)S(1)} %get-tuple-element.13.refs_1_, bf16[1,768,1536]{2,1,0:T(8,128)(2,1)S(1)} %get-tuple-element.14.refs_2_, ...), custom_call_target="tpu_custom_call" | custom-call | tf_op jit(solution)/shard_map/pallas_call | solution.py:616
